TPU v7x, 256 devices: a whole 4x4x8 slice. The times are simulated.
256 devices in a mesh: tm: 16 (over z, core), mesh: 16 (over y, x).
Axes of the slice: x: 4, y: 4, z: 8, core: 2. Of those that a mesh axis runs over, the one named last changes fastest.
Arguments:
- trajectory: bfloat16 [16, 2560, 512], P('tm', 'mesh'), may hold values from -6 to 6
- increments: bfloat16 [16, 2560, 512], P('tm', 'mesh'), may hold values from -6 to 6
- weight_send: bfloat16 [512, 512], replicated, may hold values from -0.25 to 0.25
- weight_receive: bfloat16 [512, 512], replicated, may hold values from -0.25 to 0.25
- weight_message: bfloat16 [512, 512], replicated, may hold values from -0.25 to 0.25
- weight_node: bfloat16 [512, 512], replicated, may hold values from -0.25 to 0.25
- weight_inbox: bfloat16 [512, 512], replicated, may hold values from -0.09375 to 0.09375
- weight_output: bfloat16 [512, 512], replicated, may hold values from -0.25 to 0.25
- senders: int32 [20480], P('mesh'), may hold values from 0 to 415, as said below
- receivers: int32 [20480], P('mesh'), may hold values from 0 to 159
- send_table: int32 [4096], P('mesh'), may hold values from -1 to 159, as said below
Outputs:
- forward_image: bfloat16 [16, 2560, 512], P('tm', 'mesh')
- normal_image: bfloat16 [16, 2560, 512], P('tm', 'mesh')
Inputs may be any that keep to these rules, and one draw needn't show every extreme that they name: `send_table`: entries (p * 16 + q) * 16 to (p * 16 + q + 1) * 16 - 1 list distinct local nodes of partition p needed by partition q, followed by -1 padding; a partition lists nothing to itself; every partition fills all 16 slots towards some partition and receives 16 filled slots from some partition. `senders`: values below 160 are the partition's own nodes; a value 160 + p * 16 + s names slot s of the list partition p sends to this partition, and that slot is never padding.
All inputs are finite; a program needn't handle non-finite values.
Results may differ from a plain program's by a relative error of at most 0.013.
Values may be sent and summed in bfloat16 or wider, within the bound.
A program may use at most 64 MiB of HBM per device.

v0:
```python
import jax
import jax.numpy as jnp
from jax import lax
from jax.sharding import PartitionSpec as P


def shifted(value, axis, by):
    length = lax.axis_size(axis)
    pairs = [(i, i + by) for i in range(length) if 0 <= i + by < length]
    return lax.ppermute(value, axis, pairs)


def matmul(left, right):
    return jnp.dot(left, right, preferred_element_type=jnp.float32)


def silu_slope(values):
    gate_value = jax.nn.sigmoid(values)
    return gate_value * (1.0 + values * (1.0 - gate_value))


def gather_rows(table, source):
    return matmul(table, source).astype(jnp.bfloat16)


def collect_rows(table, values):
    return lax.dot_general(
        table, values, (((0,), (0,)), ((), ())), preferred_element_type=jnp.float32
    )


def collect_exact(table, values):
    upper = values.astype(jnp.bfloat16)
    lower = (values - upper.astype(jnp.float32)).astype(jnp.bfloat16)
    return collect_rows(table, upper) + collect_rows(table, lower)


def on_device(
    trajectory,
    increments,
    weight_send,
    weight_receive,
    weight_message,
    weight_node,
    weight_inbox,
    weight_output,
    senders,
    receivers,
    send_table,
):
    state_now = trajectory[0]
    increment = increments[0]
    node_count = state_now.shape[0]
    width = state_now.shape[1]
    extended = node_count + send_table.shape[0]
    picker = (send_table[:, None] == jnp.arange(node_count, dtype=jnp.int32)[None, :]).astype(
        jnp.bfloat16
    )
    outgoing_state = matmul(picker, state_now).astype(jnp.bfloat16)
    outgoing_incr = matmul(picker, increment).astype(jnp.bfloat16)
    halo_state, halo_incr = (
        lax.all_to_all(outgoing_state, "mesh", split_axis=0, concat_axis=0, tiled=True),
        lax.all_to_all(outgoing_incr, "mesh", split_axis=0, concat_axis=0, tiled=True),
    )
    ext_both = jnp.concatenate(
        [
            jnp.concatenate([state_now, increment], axis=1),
            jnp.concatenate([halo_state, halo_incr], axis=1),
        ],
        axis=0,
    )
    own_both = jnp.concatenate([state_now, increment], axis=1)
    sender_table = (senders[:, None] == jnp.arange(extended, dtype=jnp.int32)[None, :]).astype(
        jnp.bfloat16
    )
    receiver_table = (
        receivers[:, None] == jnp.arange(node_count, dtype=jnp.int32)[None, :]
    ).astype(jnp.bfloat16)
    edge_senders = gather_rows(sender_table, ext_both)
    edge_receivers = gather_rows(receiver_table, own_both)
    pre_edge = matmul(edge_senders[:, :width], weight_send) + matmul(
        edge_receivers[:, :width], weight_receive
    )
    edge_act = jax.nn.silu(pre_edge).astype(jnp.bfloat16)
    edge_slope = silu_slope(pre_edge)
    edge_sum = collect_rows(receiver_table, edge_act).astype(jnp.bfloat16)
    inbox = matmul(edge_sum, weight_message).astype(jnp.bfloat16)
    node_slope = silu_slope(matmul(state_now, weight_node) + matmul(inbox, weight_inbox))
    edge_pre = matmul(edge_senders[:, width:], weight_send) + matmul(
        edge_receivers[:, width:], weight_receive
    )
    edge_tangent = (edge_slope * edge_pre).astype(jnp.bfloat16)
    tangent_sum = collect_rows(receiver_table, edge_tangent).astype(jnp.bfloat16)
    inbox_tangent = matmul(tangent_sum, weight_message).astype(jnp.bfloat16)
    node_tangent = (
        node_slope * (matmul(increment, weight_node) + matmul(inbox_tangent, weight_inbox))
    ).astype(jnp.bfloat16)
    tangent = (increment.astype(jnp.float32) + matmul(node_tangent, weight_output)).astype(
        jnp.bfloat16
    )
    before = shifted(tangent, "tm", 1)
    forward_image = (increment.astype(jnp.float32) - before.astype(jnp.float32)).astype(
        jnp.bfloat16
    )
    cotangent = shifted(forward_image, "tm", -1)
    node_bar = (node_slope * matmul(cotangent, weight_output.T)).astype(jnp.bfloat16)
    inbox_bar = matmul(node_bar, weight_inbox.T).astype(jnp.bfloat16)
    edge_inbox = gather_rows(receiver_table, inbox_bar)
    edge_bar = edge_slope * matmul(edge_inbox, weight_message.T)
    part_sums = collect_exact(sender_table, edge_bar).astype(jnp.bfloat16)
    recv_sums = collect_exact(receiver_table, edge_bar).astype(jnp.bfloat16)
    returned = lax.all_to_all(
        part_sums[node_count:], "mesh", split_axis=0, concat_axis=0, tiled=True
    )
    owned = (part_sums[:node_count].astype(jnp.float32) + matmul(picker.T, returned)).astype(
        jnp.bfloat16
    )
    adjoint = cotangent.astype(jnp.float32) + matmul(node_bar, weight_node.T)
    adjoint = adjoint + matmul(owned, weight_send.T) + matmul(recv_sums, weight_receive.T)
    normal_image = (forward_image.astype(jnp.float32) - adjoint).astype(jnp.bfloat16)
    return (forward_image[None], normal_image[None])


def solution(mesh):
    in_specs = (
        P("tm", "mesh", None),
        P("tm", "mesh", None),
        P(),
        P(),
        P(),
        P(),
        P(),
        P(),
        P("mesh"),
        P("mesh"),
        P("mesh"),
    )
    out_specs = (P("tm", "mesh", None), P("tm", "mesh", None))
    return jax.shard_map(
        on_device, mesh=mesh, in_specs=in_specs, out_specs=out_specs, check_vma=False
    )
```

profile of v0, /device:TPU:97, one launch (start us, length us, event | category | flops | bytes accessed | tf_op | source)
XLA Modules:
  0.0 89.7 jit_solution(12908883268905696414)
XLA Ops:
  0.6 0.0 copy-start
  0.6 0.0 copy-start.7
  0.7 2.0 %convolution_convert_fusion.4 = bf16[256,512]{1,0:T(8,128)(2,1)} fusion(s32[256]{0:T(256)} %param.21, bf16[1,160,512]{2,1,0:T(8,128)(2,1)} %param.11), kind=kOutput, calls=%fused_computation.32 | convolution fusion | flops 42115072 | bytes 427008 | tf_op jit(solution)/shard_map/dot_general | solution.py:14
  2.6 6.9 %all-to-all-start = ((bf16[16,16,512]{2,1,0:T(8,128)(2,1)}), bf16[16,16,512]{2,1,0:T(8,128)(2,1)}, u32[]{:S(2)}, u32[]{:S(2)}) async-start(bf16[16,16,512]{2,1,0:T(8,128)(2,1)} %bitcast.2), calls=%async_computation | async-start | bytes 524288 | tf_op jit(solution)/shard_map/all_to_all | solution.py:62
  9.6 0.0 copy-start.1
  9.6 2.0 %convolution_convert_fusion.3 = bf16[256,512]{1,0:T(8,128)(2,1)} fusion(s32[256]{0:T(256)} %param.21, bf16[1,160,512]{2,1,0:T(8,128)(2,1)} %param.12), kind=kOutput, calls=%fused_computation.31 | convolution fusion | flops 42115072 | bytes 427008 | tf_op jit(solution)/shard_map/dot_general | solution.py:14
  11.6 1.9 %convolution_convert_fusion = bf16[1280,1024]{1,0:T(8,128)(2,1)S(1)} fusion(s32[1280]{0:T(1024)} %param.20, bf16[160,512]{1,0:T(8,128)(2,1)} %bitcast.46, bf16[160,512]{1,0:T(8,128)(2,1)} %bitcast.48), kind=kOutput, calls=%fused_computation | convolution fusion | flops 421601280 | bytes 2954240 | tf_op jit(solution)/shard_map/dot_general | solution.py:14
  13.5 1.0 %fusion.63 = f32[160,512]{1,0:T(8,128)} fusion(bf16[512,512]{1,0:T(8,128)(2,1)S(1)} %copy-done.1, bf16[1,160,512]{2,1,0:T(8,128)(2,1)S(1)} %copy-done.7), kind=kOutput, calls=%fused_computation.82 | convolution fusion | flops 83886080 | bytes 1015808 | tf_op jit(solution)/shard_map/dot_general | solution.py:14
  14.5 2.7 %all-to-all-done = bf16[16,16,512]{2,1,0:T(8,128)(2,1)} async-done(((bf16[16,16,512]{2,1,0:T(8,128)(2,1)}), bf16[16,16,512]{2,1,0:T(8,128)(2,1)}, u32[]{:S(2)}, u32[]{:S(2)}) %all-to-all-start) | async-done | bytes 262176 | tf_op jit(solution)/shard_map/all_to_all | solution.py:62
  17.2 4.2 %all-to-all-start.1 = ((bf16[16,16,512]{2,1,0:T(8,128)(2,1)}), bf16[16,16,512]{2,1,0:T(8,128)(2,1)}, u32[]{:S(2)}, u32[]{:S(2)}) async-start(bf16[16,16,512]{2,1,0:T(8,128)(2,1)} %bitcast.51), calls=%async_computation.1 | async-start | bytes 524288 | tf_op jit(solution)/shard_map/all_to_all | solution.py:63
  21.4 0.0 copy-done.2
  21.4 2.0 %fusion.65 = f32[160,512]{1,0:T(8,128)} fusion(bf16[512,512]{1,0:T(8,128)(2,1)} %param.16, bf16[1,160,512]{2,1,0:T(8,128)(2,1)S(1)} %copy-done.2), kind=kOutput, calls=%fused_computation.84 | convolution fusion | flops 83886080 | bytes 1015808 | tf_op jit(solution)/shard_map/dot_general | solution.py:14
  23.4 5.5 %all-to-all-done.1 = bf16[16,16,512]{2,1,0:T(8,128)(2,1)} async-done(((bf16[16,16,512]{2,1,0:T(8,128)(2,1)}), bf16[16,16,512]{2,1,0:T(8,128)(2,1)}, u32[]{:S(2)}, u32[]{:S(2)}) %all-to-all-start.1) | async-done | bytes 262176 | tf_op jit(solution)/shard_map/all_to_all | solution.py:63
  28.9 2.6 %convolution_convert_fusion.1 = bf16[1280,1024]{1,0:T(8,128)(2,1)S(1)} fusion(s32[1280]{0:T(1024)S(1)} %copy-done.14, bf16[256,512]{1,0:T(8,128)(2,1)} %bitcast.5, bf16[256,512]{1,0:T(8,128)(2,1)} %bitcast.3, bf16[160,512]{1,0:T(8,128)(2,1)S(1)} %bitcast.47, bf16[160,512]{1,0:T(8,128)(2,1)S(1)} %bitcast.49), kind=kOutput, calls=%fused_computation.1 | convolution fusion | flops 1095770112 | bytes 3478528 | tf_op jit(solution)/shard_map/dot_general | solution.py:14
  31.6 0.0 copy-done
  31.6 0.8 fusion.9
  32.4 0.0 copy-start.6
  32.4 2.4 %fusion.6 = f32[1280,512]{1,0:T(8,128)} fusion(bf16[512,512]{1,0:T(8,128)(2,1)S(1)} %copy-done, bf16[1280,1024]{1,0:T(8,128)(2,1)S(1)} %convolution_convert_fusion.1), kind=kOutput, calls=%fused_computation.17 | convolution fusion | flops 671088640 | bytes 4456448 | tf_op jit(solution)/shard_map/dot_general | solution.py:14
  34.8 0.9 convolution_add_fusion.1
  35.7 1.5 %copy-done.3 = f32[1280,512]{1,0:T(8,128)} copy-done((f32[1280,512]{1,0:T(8,128)}, f32[1280,512]{1,0:T(8,128)S(1)}, u32[]{:S(2)}) %copy-start.3) | copy-done | bytes 2621464
  37.2 1.8 %fusion.28 = bf16[160,512]{1,0:T(8,128)(2,1)} fusion(f32[1280,512]{1,0:T(8,128)S(1)} %convolution_add_fusion.1, s32[1280]{0:T(1024)S(1)} %copy-done.12), kind=kOutput, calls=%fused_computation.48 | convolution fusion | flops 213278720 | bytes 2790400 | tf_op jit(solution)/shard_map/dot_general | solution.py:27
  39.0 4.4 %fusion.29 = bf16[160,512]{1,0:T(8,128)(2,1)S(1)} fusion(f32[1280,512]{1,0:T(8,128)} %fusion.6, bf16[512,512]{1,0:T(8,128)(2,1)} %param.14, bf16[1280,1024]{1,0:T(8,128)(2,1)S(1)} %convolution_convert_fusion, s32[1280]{0:T(1024)S(1)} %copy-done.12, f32[1280,512]{1,0:T(8,128)} %copy-done.3), kind=kOutput, calls=%fused_computation.49 | convolution fusion | flops 887644160 | bytes 7249920 | tf_op jit(solution)/shard_map/dot_general | solution.py:27
  43.5 0.0 copy-start.5
  43.5 0.0 copy-start.10
  43.5 0.0 copy-start.4
  43.5 2.0 %add_multiply_fusion.1 = f32[160,512]{1,0:T(8,128)S(1)} fusion(f32[160,512]{1,0:T(8,128)} %fusion.63, bf16[512,512]{1,0:T(8,128)(2,1)} %param.17, bf16[160,512]{1,0:T(8,128)(2,1)} %fusion.28, bf16[512,512]{1,0:T(8,128)(2,1)} %param.15), kind=kOutput, calls=%fused_computation.72 | convolution fusion | flops 168509440 | bytes 1867776 | tf_op jit(solution)/shard_map/dot_general | solution.py:14
  45.5 0.4 fusion.27
  46.0 0.2 fusion.23
  46.2 7.9 %collective-permute-start = (bf16[160,512]{1,0:T(8,128)(2,1)S(1)}, bf16[160,512]{1,0:T(8,128)(2,1)S(1)}, u32[]{:S(2)}, u32[]{:S(2)}) collective-permute-start(bf16[160,512]{1,0:T(8,128)(2,1)S(1)} %fusion.23), channel_id=1, source_target_pairs={{0,16},{16,32},{32,48},{48,64},{64,80},{80,96},{96,112},{112,128},... | collective-permute-start | bytes 491528 | tf_op jit(solution)/shard_map/ppermute | solution.py:10
  54.1 2.2 %collective-permute-done = bf16[160,512]{1,0:T(8,128)(2,1)S(1)} collective-permute-done((bf16[160,512]{1,0:T(8,128)(2,1)S(1)}, bf16[160,512]{1,0:T(8,128)(2,1)S(1)}, u32[]{:S(2)}, u32[]{:S(2)}) %collective-permute-start) | collective-permute-done | bytes 163872 | tf_op jit(solution)/shard_map/ppermute | solution.py:10
  56.4 0.0 copy-start.9
  56.4 2.1 %collective-permute-start.1 = (bf16[160,512]{1,0:T(8,128)(2,1)S(1)}, bf16[160,512]{1,0:T(8,128)(2,1)S(1)}, u32[]{:S(2)}, u32[]{:S(2)}) collective-permute-start(bf16[160,512]{1,0:T(8,128)(2,1)S(1)} %fusion.49), channel_id=1, source_target_pairs={{16,0},{32,16},{48,32},{64,48},{80,64},{96,80},{112,96},{128,112},... | collective-permute-start | bytes 491528 | tf_op jit(solution)/shard_map/ppermute | solution.py:10
  58.5 6.5 %collective-permute-done.1 = bf16[160,512]{1,0:T(8,128)(2,1)S(1)} collective-permute-done((bf16[160,512]{1,0:T(8,128)(2,1)S(1)}, bf16[160,512]{1,0:T(8,128)(2,1)S(1)}, u32[]{:S(2)}, u32[]{:S(2)}) %collective-permute-start.1) | collective-permute-done | bytes 163872 | tf_op jit(solution)/shard_map/ppermute | solution.py:10
  65.0 0.3 fusion.24
  65.3 0.0 copy-done.9
  65.4 1.0 %convolution_convert_fusion.5 = bf16[160,512]{1,0:T(8,128)(2,1)} fusion(bf16[160,512]{1,0:T(8,128)(2,1)S(1)} %fusion.24, bf16[512,512]{1,0:T(8,128)(2,1)S(1)} %copy-done.5), kind=kOutput, calls=%fused_computation.44 | convolution fusion | flops 83968000 | bytes 851968 | tf_op jit(solution)/shard_map/dot_general | solution.py:14
  66.4 3.7 %convolution_multiply_fusion = f32[1280,512]{1,0:T(8,128)S(1)} fusion(bf16[512,512]{1,0:T(8,128)(2,1)} %param.15, bf16[160,512]{1,0:T(8,128)(2,1)} %convolution_convert_fusion.5, s32[1280]{0:T(1024)S(1)} %copy-done.12, f32[1280,512]{1,0:T(8,128)} %copy-done.3), kind=kOutput, calls=%fused_computation.2 | convolution fusion | flops 886906880 | bytes 5936128 | tf_op jit(solution)/shard_map/dot_general | solution.py:14
  70.1 1.2 %fusion.2 = f32[416,512]{1,0:T(8,128)S(1)} fusion(s32[1280]{0:T(1024)S(1)} %copy-done.14, f32[1280,512]{1,0:T(8,128)S(1)} %convolution_multiply_fusion), kind=kOutput, calls=%fused_computation.13 | convolution fusion | flops 548413440 | bytes 3478528 | tf_op jit(solution)/shard_map/dot_general | solution.py:27
  71.3 1.5 %fusion.14 = f32[160,512]{1,0:T(8,128)} fusion(s32[1280]{0:T(1024)S(1)} %copy-done.12, f32[1280,512]{1,0:T(8,128)S(1)} %convolution_multiply_fusion), kind=kOutput, calls=%fused_computation.26 | convolution fusion | flops 212541440 | bytes 2954240 | tf_op jit(solution)/shard_map/dot_general | solution.py:27
  72.7 1.2 %fusion.18 = bf16[416,512]{1,0:T(8,128)(2,1)S(1)} fusion(f32[416,512]{1,0:T(8,128)S(1)} %fusion.2, s32[1280]{0:T(1024)S(1)} %copy-done.14, f32[1280,512]{1,0:T(8,128)S(1)} %convolution_multiply_fusion), kind=kOutput, calls=%fused_computation.30 | convolution fusion | flops 546873344 | bytes 3904512 | tf_op jit(solution)/shard_map/dot_general | solution.py:27
  74.0 0.0 copy-start.11
  74.0 0.7 copy-done.11
  74.7 0.7 slice.29
  75.4 4.3 %all-to-all-start.2 = ((bf16[16,16,512]{2,1,0:T(8,128)(2,1)}), bf16[16,16,512]{2,1,0:T(8,128)(2,1)}, u32[]{:S(2)}, u32[]{:S(2)}) async-start(bf16[16,16,512]{2,1,0:T(8,128)(2,1)} %bitcast.50), calls=%async_computation.2 | async-start | bytes 524288 | tf_op jit(solution)/shard_map/all_to_all | solution.py:112
  79.8 2.8 %fusion.33 = f32[160,512]{1,0:T(8,128)} fusion(bf16[512,512]{1,0:T(8,128)(2,1)} %param.14, f32[160,512]{1,0:T(8,128)} %fusion.14, s32[1280]{0:T(1024)S(1)} %copy-done.12, f32[1280,512]{1,0:T(8,128)S(1)} %convolution_multiply_fusion), kind=kOutput, calls=%fused_computation.51 | convolution fusion | flops 294625280 | bytes 3806208 | tf_op jit(solution)/shard_map/dot_general | solution.py:14
  82.6 1.3 %fusion.72 = f32[160,512]{1,0:T(8,128)S(1)} fusion(bf16[160,512]{1,0:T(8,128)(2,1)S(1)} %fusion.24, bf16[512,512]{1,0:T(8,128)(2,1)} %param.16), kind=kOutput, calls=%fused_computation.90 | convolution fusion | flops 83886080 | bytes 1015808 | tf_op jit(solution)/shard_map/dot_general | solution.py:14
  83.9 3.4 %all-to-all-done.2 = bf16[16,16,512]{2,1,0:T(8,128)(2,1)} async-done(((bf16[16,16,512]{2,1,0:T(8,128)(2,1)}), bf16[16,16,512]{2,1,0:T(8,128)(2,1)}, u32[]{:S(2)}, u32[]{:S(2)}) %all-to-all-start.2) | async-done | bytes 262176 | tf_op jit(solution)/shard_map/all_to_all | solution.py:112
  87.3 2.4 %fusion.54 = bf16[1,160,512]{2,1,0:T(8,128)(2,1)} fusion(f32[160,512]{1,0:T(8,128)} %fusion.33, bf16[512,512]{1,0:T(8,128)(2,1)S(1)} %copy-done, bf16[256,512]{1,0:T(8,128)(2,1)} %bitcast.8, f32[160,512]{1,0:T(8,128)S(1)} %fusion.72, bf16[160,512]{1,0:T(8,128)(2,1)S(1)} %collective-permute-done.1, bf16[160,512]{1,0:T(8,128)(2,1)} %copy-done.9, ...), kind=kOutput, calls=%fused_computation.74 | convolution fusion | flops 126689280 | bytes 2098176 | tf_op jit(solution)/shard_map/dot_general | solution.py:14
  (17 shorter events, 0.1 us)
Async XLA Ops:
  0.6 30.9 %copy-start = (bf16[512,512]{1,0:T(8,128)(2,1)S(1)}, bf16[512,512]{1,0:T(8,128)(2,1)}, u32[]{:S(2)}) copy-start(bf16[512,512]{1,0:T(8,128)(2,1)} %param.13) | copy-start | bytes 1572868
  0.6 12.8 %copy-start.7 = (bf16[1,160,512]{2,1,0:T(8,128)(2,1)S(1)}, bf16[1,160,512]{2,1,0:T(8,128)(2,1)}, u32[]{:S(2)}) copy-start(bf16[1,160,512]{2,1,0:T(8,128)(2,1)} %param.11) | copy-start | bytes 491524
  2.6 18.7 %copy-start.2 = (bf16[1,160,512]{2,1,0:T(8,128)(2,1)S(1)}, bf16[1,160,512]{2,1,0:T(8,128)(2,1)}, u32[]{:S(2)}) copy-start(bf16[1,160,512]{2,1,0:T(8,128)(2,1)} %param.12) | copy-start | bytes 491524
  2.6 14.5 %all-to-all-start = ((bf16[16,16,512]{2,1,0:T(8,128)(2,1)}), bf16[16,16,512]{2,1,0:T(8,128)(2,1)}, u32[]{:S(2)}, u32[]{:S(2)}) async-start(bf16[16,16,512]{2,1,0:T(8,128)(2,1)} %bitcast.2), calls=%async_computation | async-start | bytes 524288 | tf_op jit(solution)/shard_map/all_to_all | solution.py:62
  9.6 3.9 %copy-start.1 = (bf16[512,512]{1,0:T(8,128)(2,1)S(1)}, bf16[512,512]{1,0:T(8,128)(2,1)}, u32[]{:S(2)}) copy-start(bf16[512,512]{1,0:T(8,128)(2,1)} %param.16) | copy-start | bytes 1572868
  11.6 17.4 %copy-start.14 = (s32[1280]{0:T(1024)S(1)}, s32[1280]{0:T(1024)}, u32[]{:S(2)}) copy-start(s32[1280]{0:T(1024)} %param.19) | copy-start | bytes 15364
  17.2 11.8 %all-to-all-start.1 = ((bf16[16,16,512]{2,1,0:T(8,128)(2,1)}), bf16[16,16,512]{2,1,0:T(8,128)(2,1)}, u32[]{:S(2)}, u32[]{:S(2)}) async-start(bf16[16,16,512]{2,1,0:T(8,128)(2,1)} %bitcast.51), calls=%async_computation.1 | async-start | bytes 524288 | tf_op jit(solution)/shard_map/all_to_all | solution.py:63
  32.4 2.4 %copy-start.6 = (bf16[512,512]{1,0:T(8,128)(2,1)S(1)}, bf16[512,512]{1,0:T(8,128)(2,1)}, u32[]{:S(2)}) copy-start(bf16[512,512]{1,0:T(8,128)(2,1)} %param.14) | copy-start | bytes 1572868
  34.8 2.4 %copy-start.12 = (s32[1280]{0:T(1024)S(1)}, s32[1280]{0:T(1024)}, u32[]{:S(2)}) copy-start(s32[1280]{0:T(1024)} %param.20) | copy-start | bytes 15364
  35.7 1.5 %copy-start.3 = (f32[1280,512]{1,0:T(8,128)}, f32[1280,512]{1,0:T(8,128)S(1)}, u32[]{:S(2)}) copy-start(f32[1280,512]{1,0:T(8,128)S(1)} %convolution_add_fusion.1) | copy-start | bytes 7864324
  43.5 2.0 %copy-start.5 = (bf16[512,512]{1,0:T(8,128)(2,1)S(1)}, bf16[512,512]{1,0:T(8,128)(2,1)}, u32[]{:S(2)}) copy-start(bf16[512,512]{1,0:T(8,128)(2,1)} %param.17) | copy-start | bytes 1572868
  43.5 2.0 %copy-start.8 = (f32[160,512]{1,0:T(8,128)S(1)}, f32[160,512]{1,0:T(8,128)}, u32[]{:S(2)}) copy-start(f32[160,512]{1,0:T(8,128)} %fusion.65) | copy-start | bytes 983044
  43.5 2.0 %copy-start.10 = (bf16[512,512]{1,0:T(8,128)(2,1)S(1)}, bf16[512,512]{1,0:T(8,128)(2,1)}, u32[]{:S(2)}) copy-start(bf16[512,512]{1,0:T(8,128)(2,1)} %param.15) | copy-start | bytes 1572868
  43.5 2.5 %copy-start.4 = (bf16[512,512]{1,0:T(8,128)(2,1)S(1)}, bf16[512,512]{1,0:T(8,128)(2,1)}, u32[]{:S(2)}) copy-start(bf16[512,512]{1,0:T(8,128)(2,1)} %param.18) | copy-start | bytes 1572868
  46.2 10.1 %collective-permute-start = (bf16[160,512]{1,0:T(8,128)(2,1)S(1)}, bf16[160,512]{1,0:T(8,128)(2,1)S(1)}, u32[]{:S(2)}, u32[]{:S(2)}) collective-permute-start(bf16[160,512]{1,0:T(8,128)(2,1)S(1)} %fusion.23), channel_id=1, source_target_pairs={{0,16},{16,32},{32,48},{48,64},{64,80},{80,96},{96,112},{112,128},... | collective-permute-start | bytes 491528 | tf_op jit(solution)/shard_map/ppermute | solution.py:10
  56.4 8.9 %copy-start.9 = (bf16[160,512]{1,0:T(8,128)(2,1)}, bf16[160,512]{1,0:T(8,128)(2,1)S(1)}, u32[]{:S(2)}) copy-start(bf16[160,512]{1,0:T(8,128)(2,1)S(1)} %fusion.49) | copy-start | bytes 491524
  56.4 8.6 %collective-permute-start.1 = (bf16[160,512]{1,0:T(8,128)(2,1)S(1)}, bf16[160,512]{1,0:T(8,128)(2,1)S(1)}, u32[]{:S(2)}, u32[]{:S(2)}) collective-permute-start(bf16[160,512]{1,0:T(8,128)(2,1)S(1)} %fusion.49), channel_id=1, source_target_pairs={{16,0},{32,16},{48,32},{64,48},{80,64},{96,80},{112,96},{128,112},... | collective-permute-start | bytes 491528 | tf_op jit(solution)/shard_map/ppermute | solution.py:10
  74.0 0.8 copy-start.11
  75.4 11.9 %copy-start.13 = (s32[256]{0:T(256)S(1)}, s32[256]{0:T(256)}, u32[]{:S(2)}) copy-start(s32[256]{0:T(256)} %param.21) | copy-start | bytes 3076
  75.4 11.9 %all-to-all-start.2 = ((bf16[16,16,512]{2,1,0:T(8,128)(2,1)}), bf16[16,16,512]{2,1,0:T(8,128)(2,1)}, u32[]{:S(2)}, u32[]{:S(2)}) async-start(bf16[16,16,512]{2,1,0:T(8,128)(2,1)} %bitcast.50), calls=%async_computation.2 | async-start | bytes 524288 | tf_op jit(solution)/shard_map/all_to_all | solution.py:112
where the time goes:
time: 90.3 us; the launch traced here: 89.7 us
  matrix products  39.9 us (44%)
  starting transfers between devices  25.5 us (28%)
  waiting for transfers between devices  20.3 us (22%)
  local copies, waits for them, and re-layouts  3.02 us (3%)
  between operations  0.92 us (1%)
    dot_general x18, matrix products, matmul(): return jnp.dot(left, right, preferred_element_type=jnp.float32)  29.8 us
    dot_general x5, matrix products, collect_rows(): lax.dot_general(table, values, (((0,), (0,)), ((), ())), preferred_elemen...  10.1 us
    ppermute x2, starting transfers between devices, shifted(): return lax.ppermute(value, axis, pairs)  10 us
    ppermute x2, waiting for transfers between devices, shifted(): return lax.ppermute(value, axis, pairs)  8.73 us
    all_to_all x1, starting transfers between devices, on_device(): lax.all_to_all(outgoing_state, 'mesh', split_axis=0, concat_axis=0, tiled...  6.94 us
    all_to_all x1, waiting for transfers between devices, on_device(): lax.all_to_all(outgoing_incr, 'mesh', split_axis=0, concat_axis=0, tiled=...  5.51 us
    all_to_all x1, starting transfers between devices, on_device(): lax.all_to_all(part_sums[node_count:], 'mesh', split_axis=0, concat_axis=...  4.32 us
    all_to_all x1, starting transfers between devices, on_device(): lax.all_to_all(outgoing_incr, 'mesh', split_axis=0, concat_axis=0, tiled=...  4.19 us
  transfers between devices with their start and end apart: 5, of which 5 were waited for; matrix products, arithmetic and copies ran while one was open for 12% of the time, Pallas kernels for 0%

commit v1 on v0

v1 whole, which is shorter than its diff:
```python
import jax
import jax.numpy as jnp
from jax import lax
from jax.experimental import pallas as pl
from jax.experimental.pallas import tpu as pltpu
from jax.sharding import PartitionSpec as P

MESH = pl.DeviceIdType.MESH
F32 = jnp.float32
BF16 = jnp.bfloat16

WIDTH = 512
OWN = 160
SLOT = 16
PARTS = 16
WINDOW = 16
HALO = PARTS * SLOT
EDGES = 1280
LANES = 128

AWAY = sorted(
    [(dy, dx) for dy in range(4) for dx in range(4) if dy or dx],
    key=lambda d: -(min(d[0], 4 - d[0]) + min(d[1], 4 - d[1])),
)
SEND, RECEIVE, MESSAGE, NODE, INBOX, OUTPUT = range(6)


def dot(left, right):
    return jnp.dot(left, right, preferred_element_type=F32)


def dot_t(left, right):
    return lax.dot_general(left, right, (((1,), (1,)), ((), ())), preferred_element_type=F32)


def sigmoid(values):
    return 0.5 * jnp.tanh(0.5 * values) + 0.5


def ones_where(mask):
    return jnp.where(mask, 1.0, 0.0).astype(BF16)


def down_rows(row):
    return jnp.broadcast_to(row.astype(F32), (LANES, LANES)).T


def kernel(
    x_hbm,
    v_hbm,
    ws_hbm,
    wr_hbm,
    wm_hbm,
    wn_hbm,
    wi_hbm,
    wo_hbm,
    snd_hbm,
    rcv_hbm,
    tab_hbm,
    fi_ref,
    ni_ref,
    xv,
    w,
    snd,
    rcv,
    tab,
    pick,
    pick_t,
    near,
    far,
    near_t,
    far_t,
    out_x,
    out_v,
    halo_x,
    halo_v,
    inc_next,
    tan_out,
    before,
    ret_out,
    ret_in,
    loc_x,
    loc_v,
    slope,
    act,
    load_sem,
    send_sem,
    recv_sem,
):
    me = lax.axis_index("mesh")
    k = lax.axis_index("tm")
    row, col = me // 4, lax.rem(me, 4)
    peers = [
        {"mesh": lax.rem(row + dy, 4) * 4 + lax.rem(col + dx, 4)} for dy, dx in AWAY
    ]
    after = {"tm": lax.rem(k + 1, WINDOW)}
    ahead = {"tm": lax.rem(k + WINDOW - 1, WINDOW)}

    barrier = pltpu.get_barrier_semaphore()
    for peer in peers + [after, ahead]:
        pl.semaphore_signal(barrier, inc=1, device_id=peer, device_id_type=MESH)

    loads = []
    pairs = [
        (tab_hbm, tab),
        (x_hbm.at[0], xv.at[pl.ds(0, OWN)]),
        (v_hbm.at[0], xv.at[pl.ds(OWN, OWN)]),
        (ws_hbm, w.at[SEND]),
        (snd_hbm, snd),
        (rcv_hbm, rcv),
        (wr_hbm, w.at[RECEIVE]),
        (wn_hbm, w.at[NODE]),
        (wm_hbm, w.at[MESSAGE]),
        (wi_hbm, w.at[INBOX]),
        (wo_hbm, w.at[OUTPUT]),
    ]
    for at, (src, dst) in enumerate(pairs):
        load = pltpu.make_async_copy(src, dst, load_sem.at[at])
        load.start()
        loads.append(load)

    loads[0].wait()
    lane = lax.broadcasted_iota(jnp.int32, (LANES, LANES), 1).astype(F32)
    for b in range(HALO // LANES):
        rows = pl.ds(b * LANES, LANES)
        column = down_rows(tab[b : b + 1, :])
        pick[rows, 0:LANES] = ones_where(column == lane)
        pick[rows, LANES:OWN] = ones_where(column[:, : OWN - LANES] == lane[:, : OWN - LANES] + LANES)
        pick_t[:, b * LANES : (b + 1) * LANES] = ones_where(
            jnp.broadcast_to(tab[b : b + 1, :], (OWN, LANES))
            == lax.broadcasted_iota(jnp.int32, (OWN, LANES), 0)
        )
    own_rows = pl.ds(pl.multiple_of(me * SLOT, SLOT), SLOT)
    nothing = jnp.zeros((SLOT, WIDTH), BF16)
    halo_x[own_rows, :] = nothing
    halo_v[own_rows, :] = nothing
    ret_in[own_rows, :] = nothing
    for load in loads[1:4]:
        load.wait()
    sent = dot(xv[...], w[SEND]).astype(BF16)
    out_x[...] = dot(pick[...], sent[:OWN]).astype(BF16)
    out_v[...] = dot(pick[...], sent[OWN:]).astype(BF16)

    def exchange(src, dst, at):
        for peer in peers:
            there = pl.ds(pl.multiple_of(peer["mesh"] * SLOT, SLOT), SLOT)
            pltpu.make_async_remote_copy(
                src_ref=src.at[there],
                dst_ref=dst.at[own_rows],
                send_sem=send_sem.at[at],
                recv_sem=recv_sem.at[at],
                device_id=peer,
                device_id_type=MESH,
            ).start()

    def whole(src, dst, at):
        rows = pl.ds(0, HALO - SLOT)
        return pltpu.make_async_remote_copy(
            src_ref=src.at[rows],
            dst_ref=dst.at[rows],
            send_sem=send_sem.at[at],
            recv_sem=recv_sem.at[at],
            device_id=peers[0],
            device_id_type=MESH,
        )

    pl.semaphore_wait(barrier, len(peers) + 2)
    exchange(out_x, halo_x, 0)
    exchange(out_v, halo_v, 1)
    to_ahead = pltpu.make_async_remote_copy(
        src_ref=xv.at[pl.ds(OWN, OWN)],
        dst_ref=inc_next,
        send_sem=send_sem.at[3],
        recv_sem=recv_sem.at[3],
        device_id=ahead,
        device_id_type=MESH,
    )
    to_ahead.start()

    loads[4].wait()
    loads[5].wait()
    for b in range(EDGES // LANES):
        rows = pl.ds(b * LANES, LANES)
        cols = slice(b * LANES, (b + 1) * LANES)
        s_row, r_row = snd[b : b + 1, :], rcv[b : b + 1, :]
        s_col, r_col = down_rows(s_row), down_rows(r_row) + OWN
        near[rows, 0:LANES] = ones_where(s_col == lane)
        near[rows, LANES : 2 * LANES] = ones_where(
            jnp.where(lane < OWN - LANES, s_col, r_col) == lane + LANES
        )
        near[rows, 2 * LANES : 2 * OWN] = ones_where(
            (r_col == lane + 2 * LANES)[:, : 2 * OWN - 2 * LANES]
        )
        far[rows, 0:LANES] = ones_where(s_col == lane + OWN)
        far[rows, LANES:HALO] = ones_where(s_col == lane + (OWN + LANES))
        place = lax.broadcasted_iota(jnp.int32, (OWN, LANES), 0)
        near_t[0:OWN, cols] = ones_where(jnp.broadcast_to(s_row, (OWN, LANES)) == place)
        near_t[OWN:, cols] = ones_where(jnp.broadcast_to(r_row, (OWN, LANES)) == place)
        far_t[:, cols] = ones_where(
            jnp.broadcast_to(s_row, (HALO, LANES))
            == lax.broadcasted_iota(jnp.int32, (HALO, LANES), 0) + OWN
        )

    loads[6].wait()
    received = dot(xv[...], w[RECEIVE]).astype(BF16)
    loc_x[...] = dot(near[...], jnp.concatenate([sent[:OWN], received[:OWN]], axis=0))
    loc_v[...] = dot(near[...], jnp.concatenate([sent[OWN:], received[OWN:]], axis=0))
    for load in loads[7:]:
        load.wait()
    node = dot(xv[...], w[NODE])
    w_mi = dot(w[MESSAGE], w[INBOX]).astype(BF16)
    w_oo = dot_t(w[OUTPUT], w[OUTPUT]).astype(BF16)

    whole(out_x, halo_x, 0).wait_recv()
    pre = loc_x[...] + dot(far[...], halo_x[...])
    gate = sigmoid(pre)
    gated = pre * gate
    act[...] = gated.astype(BF16)
    slope[...] = gate + gated * (1.0 - gate)
    edge_sum = dot(near_t[OWN:, :], act[...]).astype(BF16)
    pre_node = node[:OWN] + dot(edge_sum, w_mi)
    gate_node = sigmoid(pre_node)
    node_slope = gate_node + pre_node * gate_node * (1.0 - gate_node)

    to_ahead.wait_recv()
    increment = xv[OWN:, :].astype(F32)
    step = (inc_next[...].astype(F32) - increment).astype(BF16)
    step_bar = dot_t(step, w[OUTPUT])

    whole(out_v, halo_v, 1).wait_recv()
    act[...] = (slope[...] * (loc_v[...] + dot(far[...], halo_v[...]))).astype(BF16)
    tangent_sum = dot(near_t[OWN:, :], act[...]).astype(BF16)
    node_tangent = (node_slope * (node[OWN:] + dot(tangent_sum, w_mi))).astype(BF16)
    node_bar = node_slope * (step_bar - dot(node_tangent, w_oo))
    node_bar = jnp.where(k == WINDOW - 1, 0.0, node_bar).astype(BF16)
    edge_in = dot_t(node_bar, w_mi).astype(BF16)
    act[...] = (slope[...] * dot(near[:, OWN:], edge_in)).astype(BF16)
    ret_out[...] = dot(far_t[...], act[...]).astype(BF16)
    exchange(ret_out, ret_in, 2)

    tangent = (increment + dot(node_tangent, w[OUTPUT])).astype(BF16)
    tan_out[...] = tangent
    to_after = pltpu.make_async_remote_copy(
        src_ref=tan_out,
        dst_ref=before,
        send_sem=send_sem.at[4],
        recv_sem=recv_sem.at[4],
        device_id=after,
        device_id_type=MESH,
    )
    to_after.start()

    sums = dot(near_t[...], act[...])
    cotangent = (inc_next[...].astype(F32) - tangent.astype(F32)).astype(BF16).astype(F32)
    adjoint = jnp.where(k == WINDOW - 1, 0.0, cotangent)
    adjoint = adjoint + dot_t(node_bar, w[NODE]) + dot_t(sums[OWN:].astype(BF16), w[RECEIVE])

    to_after.wait_recv()
    shifted = jnp.where(k == 0, 0.0, before[...].astype(F32))
    forward = (increment - shifted).astype(BF16)
    fi_ref[0] = forward
    rest = forward.astype(F32) - adjoint

    whole(ret_out, ret_in, 2).wait_recv()
    owned = (sums[:OWN] + dot(pick_t[...], ret_in[...])).astype(BF16)
    ni_ref[0] = (rest - dot_t(owned, w[SEND])).astype(BF16)

    whole(out_x, halo_x, 0).wait_send()
    whole(out_v, halo_v, 1).wait_send()
    whole(ret_out, ret_in, 2).wait_send()
    to_ahead.wait_send()
    to_after.wait_send()


def on_device(
    trajectory,
    increments,
    weight_send,
    weight_receive,
    weight_message,
    weight_node,
    weight_inbox,
    weight_output,
    senders,
    receivers,
    send_table,
):
    block = jax.ShapeDtypeStruct((1, OWN, WIDTH), BF16)
    rows = lambda n: pltpu.VMEM((n, WIDTH), BF16)
    return pl.pallas_call(
        kernel,
        out_shape=(block, block),
        in_specs=[pl.BlockSpec(memory_space=pltpu.HBM)] * 11,
        out_specs=(pl.BlockSpec(memory_space=pltpu.VMEM),) * 2,
        scratch_shapes=[
            rows(2 * OWN),
            pltpu.VMEM((6, WIDTH, WIDTH), BF16),
            pltpu.VMEM((EDGES // LANES, LANES), jnp.int32),
            pltpu.VMEM((EDGES // LANES, LANES), jnp.int32),
            pltpu.VMEM((HALO // LANES, LANES), jnp.int32),
            pltpu.VMEM((HALO, OWN), BF16),
            pltpu.VMEM((OWN, HALO), BF16),
            pltpu.VMEM((EDGES, 2 * OWN), BF16),
            pltpu.VMEM((EDGES, HALO), BF16),
            pltpu.VMEM((2 * OWN, EDGES), BF16),
            pltpu.VMEM((HALO, EDGES), BF16),
            rows(HALO),
            rows(HALO),
            rows(HALO),
            rows(HALO),
            rows(OWN),
            rows(OWN),
            rows(OWN),
            rows(HALO),
            rows(HALO),
            pltpu.VMEM((EDGES, WIDTH), F32),
            pltpu.VMEM((EDGES, WIDTH), F32),
            pltpu.VMEM((EDGES, WIDTH), F32),
            pltpu.VMEM((EDGES, WIDTH), BF16),
            pltpu.SemaphoreType.DMA((11,)),
            pltpu.SemaphoreType.DMA((5,)),
            pltpu.SemaphoreType.DMA((5,)),
        ],
        compiler_params=pltpu.CompilerParams(
            collective_id=0, has_side_effects=True, vmem_limit_bytes=60 << 20
        ),
    )(
        trajectory,
        increments,
        weight_send,
        weight_receive,
        weight_message,
        weight_node,
        weight_inbox,
        weight_output,
        senders.reshape(EDGES // LANES, LANES),
        receivers.reshape(EDGES // LANES, LANES),
        send_table.reshape(HALO // LANES, LANES),
    )


def solution(mesh):
    nodes = P("tm", "mesh", None)
    in_specs = (nodes, nodes) + (P(),) * 6 + (P("mesh"),) * 3
    return jax.shard_map(
        on_device, mesh=mesh, in_specs=in_specs, out_specs=(nodes, nodes), check_vma=False
    )
```

time: 90.3 us -> 27.4 us (0.30)
  the two profiles are of different devices: /device:TPU:97 before, /device:TPU:6 now
where the time goes in v1:
time: 27.4 us
  Pallas kernels  24.4 us (89%)
  local copies, waits for them, and re-layouts  2.3 us (8%)
  between operations  0.65 us (2%)
    pallas_call x1, Pallas kernels, on_device(): pl.pallas_call(kernel, out_shape=(block, block), in_specs=[pl.BlockSpec(m...  24.4 us
    unnamed x4, local copies, waits for them, and re-layouts  2.3 us

profile of v1, /device:TPU:6, one launch (start us, length us, event | category | flops | bytes accessed | tf_op | source)
XLA Modules:
  0.0 27.4 jit_solution(6661888124931922398)
XLA Ops:
  0.6 24.4 %shard_map.122 = (bf16[1,160,512]{2,1,0:T(8,128)(2,1)}, bf16[1,160,512]{2,1,0:T(8,128)(2,1)}) custom-call(bf16[1,160,512]{2,1,0:T(8,128)(2,1)} %x_hbm.1, bf16[1,160,512]{2,1,0:T(8,128)(2,1)} %v_hbm.1, bf16[512,512]{1,0:T(8,128)(2,1)} %ws_hbm.1, bf16[512,512]{1,0:T(8,128)(2,1)} %wr_hbm.1, bf16[512,512]{1,0:T(8,128)(2,1)} %wm_hbm.1, bf16[512,512]{1,0:T(8,128)(2,1)} %wn_hbm.1, ...), custom_call_target="tpu_custom_call" | custom-call | tf_op jit(solution)/shard_map/pallas_call | solution.py:290
  25.0 0.0 copy-start
  25.1 1.6 %copy.15 = bf16[1,160,512]{2,1,0:T(8,128)(2,1)} copy(bf16[1,160,512]{2,1,0:T(8,128)(2,1)} %get-tuple-element.4) | data formatting | bytes 327680
  26.7 0.0 copy-done
  26.7 0.7 %copy.16 = bf16[1,160,512]{2,1,0:T(8,128)(2,1)} copy(bf16[1,160,512]{2,1,0:T(8,128)(2,1)S(1)} %copy-done) | data formatting | bytes 327680
Async XLA Ops:
  25.0 1.6 %copy-start = (bf16[1,160,512]{2,1,0:T(8,128)(2,1)S(1)}, bf16[1,160,512]{2,1,0:T(8,128)(2,1)}, u32[]{:S(2)}) copy-start(bf16[1,160,512]{2,1,0:T(8,128)(2,1)} %get-tuple-element.5) | copy-start | bytes 491524

commit v2 on v1

--- a/solution.py
+++ b/solution.py
@@ -90,15 +90,22 @@
     me = lax.axis_index("mesh")
     k = lax.axis_index("tm")
     row, col = me // 4, lax.rem(me, 4)
-    peers = [
-        {"mesh": lax.rem(row + dy, 4) * 4 + lax.rem(col + dx, 4)} for dy, dx in AWAY
-    ]
+    targets = [lax.rem(row + dy, 4) * 4 + lax.rem(col + dx, 4) for dy, dx in AWAY]
+    sources = [lax.rem(row + 4 - dy, 4) * 4 + lax.rem(col + 4 - dx, 4) for dy, dx in AWAY]
+    first, last = k == 0, k == WINDOW - 1
     after = {"tm": lax.rem(k + 1, WINDOW)}
     ahead = {"tm": lax.rem(k + WINDOW - 1, WINDOW)}
 
     barrier = pltpu.get_barrier_semaphore()
-    for peer in peers + [after, ahead]:
+
+    def greet(peer):
         pl.semaphore_signal(barrier, inc=1, device_id=peer, device_id_type=MESH)
+
+    for target in targets:
+        greet({"mesh": target})
+    pl.when(jnp.logical_not(last))(lambda: greet(after))
+    pl.when(jnp.logical_not(first))(lambda: greet(ahead))
+    greeted = len(AWAY) + 2 - first.astype(jnp.int32) - last.astype(jnp.int32)
 
     loads = []
     pairs = [
@@ -132,53 +139,76 @@
         )
     own_rows = pl.ds(pl.multiple_of(me * SLOT, SLOT), SLOT)
     nothing = jnp.zeros((SLOT, WIDTH), BF16)
-    halo_x[own_rows, :] = nothing
-    halo_v[own_rows, :] = nothing
+    halo_x[HALO - SLOT :, :] = nothing
+    halo_v[HALO - SLOT :, :] = nothing
     ret_in[own_rows, :] = nothing
+
+    @pl.when(first)
+    def _():
+        before[...] = jnp.zeros_like(before)
+
+    @pl.when(last)
+    def _():
+        inc_next[...] = jnp.zeros_like(inc_next)
+
     for load in loads[1:4]:
         load.wait()
     sent = dot(xv[...], w[SEND]).astype(BF16)
     out_x[...] = dot(pick[...], sent[:OWN]).astype(BF16)
     out_v[...] = dot(pick[...], sent[OWN:]).astype(BF16)
 
-    def exchange(src, dst, at):
-        for peer in peers:
-            there = pl.ds(pl.multiple_of(peer["mesh"] * SLOT, SLOT), SLOT)
-            pltpu.make_async_remote_copy(
-                src_ref=src.at[there],
-                dst_ref=dst.at[own_rows],
-                send_sem=send_sem.at[at],
-                recv_sem=recv_sem.at[at],
-                device_id=peer,
-                device_id_type=MESH,
-            ).start()
-
-    def whole(src, dst, at):
-        rows = pl.ds(0, HALO - SLOT)
-        return pltpu.make_async_remote_copy(
-            src_ref=src.at[rows],
-            dst_ref=dst.at[rows],
+    def send(src, dst, at, peer):
+        pltpu.make_async_remote_copy(
+            src_ref=src,
+            dst_ref=dst,
             send_sem=send_sem.at[at],
             recv_sem=recv_sem.at[at],
-            device_id=peers[0],
+            device_id=peer,
+            device_id_type=MESH,
+        ).start()
+
+    def part(ref, p):
+        return ref.at[pl.ds(pl.multiple_of(p * SLOT, SLOT), SLOT)]
+
+    def block(ref, b):
+        return ref.at[pl.ds(b * SLOT, SLOT)]
+
+    def whole(src, dst, at):
+        return pltpu.make_async_remote_copy(
+            src_ref=src,
+            dst_ref=dst,
+            send_sem=send_sem.at[at],
+            recv_sem=recv_sem.at[at],
+            device_id={"mesh": targets[0]},
             device_id_type=MESH,
         )
 
-    pl.semaphore_wait(barrier, len(peers) + 2)
-    exchange(out_x, halo_x, 0)
-    exchange(out_v, halo_v, 1)
-    to_ahead = pltpu.make_async_remote_copy(
-        src_ref=xv.at[pl.ds(OWN, OWN)],
-        dst_ref=inc_next,
-        send_sem=send_sem.at[3],
-        recv_sem=recv_sem.at[3],
-        device_id=ahead,
-        device_id_type=MESH,
-    )
-    to_ahead.start()
+    bulk = pl.ds(0, HALO - SLOT)
+    all_x = whole(out_x.at[bulk], halo_x.at[bulk], 0)
+    all_v = whole(out_v.at[bulk], halo_v.at[bulk], 1)
+    all_back = whole(ret_out.at[bulk], ret_in.at[bulk], 2)
+    all_inc = whole(xv.at[pl.ds(OWN, OWN)], inc_next, 3)
+    all_tan = whole(tan_out, before, 4)
+
+    pl.semaphore_wait(barrier, greeted)
+    for src, dst, at in ((out_x, halo_x, 0), (out_v, halo_v, 1)):
+        for b, target in enumerate(targets):
+            send(part(src, target), block(dst, b), at, {"mesh": target})
+
+    @pl.when(jnp.logical_not(first))
+    def _():
+        send(xv.at[pl.ds(OWN, OWN)], inc_next, 3, ahead)
 
     loads[4].wait()
     loads[5].wait()
+    step16 = lax.broadcasted_iota(jnp.int32, (1, LANES), 1)
+    far_keys = []
+    for at in range(0, HALO, LANES):
+        keys = jnp.full((1, LANES), -1, jnp.int32)
+        for b in range(at // SLOT, min((at + LANES) // SLOT, len(AWAY))):
+            inside = (step16 >= b * SLOT - at) & (step16 < (b + 1) * SLOT - at)
+            keys = jnp.where(inside, step16 + (at - b * SLOT + OWN + sources[b] * SLOT), keys)
+        far_keys.append(keys.astype(F32))
     for b in range(EDGES // LANES):
         rows = pl.ds(b * LANES, LANES)
         cols = slice(b * LANES, (b + 1) * LANES)
@@ -191,15 +221,15 @@
         near[rows, 2 * LANES : 2 * OWN] = ones_where(
             (r_col == lane + 2 * LANES)[:, : 2 * OWN - 2 * LANES]
         )
-        far[rows, 0:LANES] = ones_where(s_col == lane + OWN)
-        far[rows, LANES:HALO] = ones_where(s_col == lane + (OWN + LANES))
+        for at, keys in enumerate(far_keys):
+            far[rows, at * LANES : (at + 1) * LANES] = ones_where(s_col == keys)
         place = lax.broadcasted_iota(jnp.int32, (OWN, LANES), 0)
         near_t[0:OWN, cols] = ones_where(jnp.broadcast_to(s_row, (OWN, LANES)) == place)
         near_t[OWN:, cols] = ones_where(jnp.broadcast_to(r_row, (OWN, LANES)) == place)
-        far_t[:, cols] = ones_where(
-            jnp.broadcast_to(s_row, (HALO, LANES))
-            == lax.broadcasted_iota(jnp.int32, (HALO, LANES), 0) + OWN
-        )
+        offset = jnp.broadcast_to(s_row, (SLOT, LANES)) - place[:SLOT] - OWN
+        for at, source in enumerate(sources):
+            far_t[at * SLOT : (at + 1) * SLOT, cols] = ones_where(offset == source * SLOT)
+        far_t[HALO - SLOT :, cols] = jnp.zeros((SLOT, LANES), BF16)
 
     loads[6].wait()
     received = dot(xv[...], w[RECEIVE]).astype(BF16)
@@ -211,7 +241,7 @@
     w_mi = dot(w[MESSAGE], w[INBOX]).astype(BF16)
     w_oo = dot_t(w[OUTPUT], w[OUTPUT]).astype(BF16)
 
-    whole(out_x, halo_x, 0).wait_recv()
+    all_x.wait_recv()
     pre = loc_x[...] + dot(far[...], halo_x[...])
     gate = sigmoid(pre)
     gated = pre * gate
@@ -222,54 +252,62 @@
     gate_node = sigmoid(pre_node)
     node_slope = gate_node + pre_node * gate_node * (1.0 - gate_node)
 
-    to_ahead.wait_recv()
+    pl.when(jnp.logical_not(last))(all_inc.wait_recv)
     increment = xv[OWN:, :].astype(F32)
     step = (inc_next[...].astype(F32) - increment).astype(BF16)
     step_bar = dot_t(step, w[OUTPUT])
 
-    whole(out_v, halo_v, 1).wait_recv()
+    all_v.wait_recv()
     act[...] = (slope[...] * (loc_v[...] + dot(far[...], halo_v[...]))).astype(BF16)
     tangent_sum = dot(near_t[OWN:, :], act[...]).astype(BF16)
     node_tangent = (node_slope * (node[OWN:] + dot(tangent_sum, w_mi))).astype(BF16)
     node_bar = node_slope * (step_bar - dot(node_tangent, w_oo))
-    node_bar = jnp.where(k == WINDOW - 1, 0.0, node_bar).astype(BF16)
+    node_bar = jnp.where(last, 0.0, node_bar).astype(BF16)
     edge_in = dot_t(node_bar, w_mi).astype(BF16)
     act[...] = (slope[...] * dot(near[:, OWN:], edge_in)).astype(BF16)
-    ret_out[...] = dot(far_t[...], act[...]).astype(BF16)
-    exchange(ret_out, ret_in, 2)
+    half = HALO // 2
+    for at in (0, half):
+        ret_out[at : at + half, :] = dot(far_t[at : at + half, :], act[...]).astype(BF16)
+        for b in range(at // SLOT, min((at + half) // SLOT, len(AWAY))):
+            send(block(ret_out, b), part(ret_in, me), 2, {"mesh": sources[b]})
 
     tangent = (increment + dot(node_tangent, w[OUTPUT])).astype(BF16)
     tan_out[...] = tangent
-    to_after = pltpu.make_async_remote_copy(
-        src_ref=tan_out,
-        dst_ref=before,
-        send_sem=send_sem.at[4],
-        recv_sem=recv_sem.at[4],
-        device_id=after,
-        device_id_type=MESH,
-    )
-    to_after.start()
+
+    @pl.when(jnp.logical_not(last))
+    def _():
+        send(tan_out, before, 4, after)
 
     sums = dot(near_t[...], act[...])
     cotangent = (inc_next[...].astype(F32) - tangent.astype(F32)).astype(BF16).astype(F32)
-    adjoint = jnp.where(k == WINDOW - 1, 0.0, cotangent)
+    adjoint = jnp.where(last, 0.0, cotangent)
     adjoint = adjoint + dot_t(node_bar, w[NODE]) + dot_t(sums[OWN:].astype(BF16), w[RECEIVE])
 
-    to_after.wait_recv()
-    shifted = jnp.where(k == 0, 0.0, before[...].astype(F32))
-    forward = (increment - shifted).astype(BF16)
+    pl.when(jnp.logical_not(first))(all_tan.wait_recv)
+    forward = (increment - before[...].astype(F32)).astype(BF16)
     fi_ref[0] = forward
     rest = forward.astype(F32) - adjoint
 
-    whole(ret_out, ret_in, 2).wait_recv()
+    all_back.wait_recv()
     owned = (sums[:OWN] + dot(pick_t[...], ret_in[...])).astype(BF16)
     ni_ref[0] = (rest - dot_t(owned, w[SEND])).astype(BF16)
 
-    whole(out_x, halo_x, 0).wait_send()
-    whole(out_v, halo_v, 1).wait_send()
-    whole(ret_out, ret_in, 2).wait_send()
-    to_ahead.wait_send()
-    to_after.wait_send()
+    all_x.wait_send()
+    all_v.wait_send()
+    all_back.wait_send()
+    pl.when(jnp.logical_not(first))(all_inc.wait_send)
+    pl.when(jnp.logical_not(last))(all_tan.wait_send)
+
+
+def store(fi_vmem, ni_vmem, fi_hbm, ni_hbm, sem):
+    copies = [
+        pltpu.make_async_copy(fi_vmem, fi_hbm, sem.at[0]),
+        pltpu.make_async_copy(ni_vmem, ni_hbm, sem.at[1]),
+    ]
+    for copy in copies:
+        copy.start()
+    for copy in copies:
+        copy.wait()
 
 
 def on_device(
@@ -285,12 +323,25 @@
     receivers,
     send_table,
 ):
-    block = jax.ShapeDtypeStruct((1, OWN, WIDTH), BF16)
+    image = jax.ShapeDtypeStruct((1, OWN, WIDTH), BF16)
     rows = lambda n: pltpu.VMEM((n, WIDTH), BF16)
-    return pl.pallas_call(
+    operands = (
+        trajectory,
+        increments,
+        weight_send,
+        weight_receive,
+        weight_message,
+        weight_node,
+        weight_inbox,
+        weight_output,
+        senders.reshape(EDGES // LANES, LANES),
+        receivers.reshape(EDGES // LANES, LANES),
+        send_table.reshape(HALO // LANES, LANES),
+    )
+    images = pl.pallas_call(
         kernel,
-        out_shape=(block, block),
-        in_specs=[pl.BlockSpec(memory_space=pltpu.HBM)] * 11,
+        out_shape=(pltpu.VMEM(image.shape, BF16),) * 2,
+        in_specs=[pl.BlockSpec(memory_space=pl.ANY)] * 11,
         out_specs=(pl.BlockSpec(memory_space=pltpu.VMEM),) * 2,
         scratch_shapes=[
             rows(2 * OWN),
@@ -322,21 +373,17 @@
             pltpu.SemaphoreType.DMA((5,)),
         ],
         compiler_params=pltpu.CompilerParams(
-            collective_id=0, has_side_effects=True, vmem_limit_bytes=60 << 20
+            collective_id=0, has_side_effects=True, vmem_limit_bytes=40 << 20
         ),
-    )(
-        trajectory,
-        increments,
-        weight_send,
-        weight_receive,
-        weight_message,
-        weight_node,
-        weight_inbox,
-        weight_output,
-        senders.reshape(EDGES // LANES, LANES),
-        receivers.reshape(EDGES // LANES, LANES),
-        send_table.reshape(HALO // LANES, LANES),
-    )
+    )(*[pltpu.with_memory_space_constraint(operand, pltpu.HBM) for operand in operands])
+    return pl.pallas_call(
+        store,
+        out_shape=(image, image),
+        in_specs=[pl.BlockSpec(memory_space=pltpu.VMEM)] * 2,
+        out_specs=(pl.BlockSpec(memory_space=pl.ANY),) * 2,
+        scratch_shapes=[pltpu.SemaphoreType.DMA((2,))],
+        compiler_params=pltpu.CompilerParams(vmem_limit_bytes=4 << 20),
+    )(*images)
 
 
 def solution(mesh):

time: 27.4 us -> 23.7 us (0.86)
  the two profiles are of different devices: /device:TPU:6 before, /device:TPU:96 now
where the time goes in v2:
time: 23.7 us
  Pallas kernels  23 us (97%)
  between operations  0.64 us (3%)
    pallas_call x1, Pallas kernels, on_device(): pl.pallas_call(kernel, out_shape=(pltpu.VMEM(image.shape, BF16),) * 2, in...  22.3 us
    pallas_call x1, Pallas kernels, on_device(): pl.pallas_call(store, out_shape=(image, image), in_specs=[pl.BlockSpec(me...  0.74 us

profile of v2, /device:TPU:96, one launch (start us, length us, event | category | flops | bytes accessed | tf_op | source)
XLA Modules:
  0.0 23.7 jit_solution(5137655673262330405)
XLA Ops:
  0.6 22.3 %shard_map.122 = (bf16[1,160,512]{2,1,0:T(8,128)(2,1)S(1)}, bf16[1,160,512]{2,1,0:T(8,128)(2,1)S(1)}) custom-call(bf16[1,160,512]{2,1,0:T(8,128)(2,1)} %x_hbm.1, bf16[1,160,512]{2,1,0:T(8,128)(2,1)} %v_hbm.1, bf16[512,512]{1,0:T(8,128)(2,1)} %ws_hbm.1, bf16[512,512]{1,0:T(8,128)(2,1)} %wr_hbm.1, bf16[512,512]{1,0:T(8,128)(2,1)} %wm_hbm.1, ...), custom_call_target="tpu_custom_call" | custom-call | tf_op jit(solution)/shard_map/pallas_call | solution.py:341
  22.9 0.7 %shard_map.123 = (bf16[1,160,512]{2,1,0:T(8,128)(2,1)}, bf16[1,160,512]{2,1,0:T(8,128)(2,1)}) custom-call(bf16[1,160,512]{2,1,0:T(8,128)(2,1)S(1)} %get-tuple-element.4.fi_vmem, bf16[1,160,512]{2,1,0:T(8,128)(2,1)S(1)} %get-tuple-element.5.ni_vmem), custom_call_target="tpu_custom_call" | custom-call | tf_op jit(solution)/shard_map/pallas_call | solution.py:379

commit v3 on v2

--- a/solution.py
+++ b/solution.py
@@ -61,8 +61,7 @@
     ni_ref,
     xv,
     w,
-    snd,
-    rcv,
+    ends,
     tab,
     pick,
     pick_t,
@@ -107,24 +106,25 @@
     pl.when(jnp.logical_not(first))(lambda: greet(ahead))
     greeted = len(AWAY) + 2 - first.astype(jnp.int32) - last.astype(jnp.int32)
 
+    groups = [
+        (tab, [(tab_hbm, tab)]),
+        (xv, [(x_hbm.at[0], xv.at[pl.ds(0, OWN)]), (v_hbm.at[0], xv.at[pl.ds(OWN, OWN)])]),
+        (w.at[SEND], [(ws_hbm, w.at[SEND])]),
+        (ends, [(snd_hbm, ends.at[0]), (rcv_hbm, ends.at[1])]),
+        (w.at[RECEIVE], [(wr_hbm, w.at[RECEIVE])]),
+        (
+            w.at[pl.ds(MESSAGE, 4)],
+            [
+                (hbm, w.at[at])
+                for at, hbm in ((NODE, wn_hbm), (MESSAGE, wm_hbm), (INBOX, wi_hbm), (OUTPUT, wo_hbm))
+            ],
+        ),
+    ]
     loads = []
-    pairs = [
-        (tab_hbm, tab),
-        (x_hbm.at[0], xv.at[pl.ds(0, OWN)]),
-        (v_hbm.at[0], xv.at[pl.ds(OWN, OWN)]),
-        (ws_hbm, w.at[SEND]),
-        (snd_hbm, snd),
-        (rcv_hbm, rcv),
-        (wr_hbm, w.at[RECEIVE]),
-        (wn_hbm, w.at[NODE]),
-        (wm_hbm, w.at[MESSAGE]),
-        (wi_hbm, w.at[INBOX]),
-        (wo_hbm, w.at[OUTPUT]),
-    ]
-    for at, (src, dst) in enumerate(pairs):
-        load = pltpu.make_async_copy(src, dst, load_sem.at[at])
-        load.start()
-        loads.append(load)
+    for at, (whole_group, pairs) in enumerate(groups):
+        for src, dst in pairs:
+            pltpu.make_async_copy(src, dst, load_sem.at[at]).start()
+        loads.append(pltpu.make_async_copy(whole_group, whole_group, load_sem.at[at]))
 
     loads[0].wait()
     lane = lax.broadcasted_iota(jnp.int32, (LANES, LANES), 1).astype(F32)
@@ -151,8 +151,8 @@
     def _():
         inc_next[...] = jnp.zeros_like(inc_next)
 
-    for load in loads[1:4]:
-        load.wait()
+    loads[1].wait()
+    loads[2].wait()
     sent = dot(xv[...], w[SEND]).astype(BF16)
     out_x[...] = dot(pick[...], sent[:OWN]).astype(BF16)
     out_v[...] = dot(pick[...], sent[OWN:]).astype(BF16)
@@ -199,8 +199,7 @@
     def _():
         send(xv.at[pl.ds(OWN, OWN)], inc_next, 3, ahead)
 
-    loads[4].wait()
-    loads[5].wait()
+    loads[3].wait()
     step16 = lax.broadcasted_iota(jnp.int32, (1, LANES), 1)
     far_keys = []
     for at in range(0, HALO, LANES):
@@ -212,7 +211,7 @@
     for b in range(EDGES // LANES):
         rows = pl.ds(b * LANES, LANES)
         cols = slice(b * LANES, (b + 1) * LANES)
-        s_row, r_row = snd[b : b + 1, :], rcv[b : b + 1, :]
+        s_row, r_row = ends[0, b : b + 1, :], ends[1, b : b + 1, :]
         s_col, r_col = down_rows(s_row), down_rows(r_row) + OWN
         near[rows, 0:LANES] = ones_where(s_col == lane)
         near[rows, LANES : 2 * LANES] = ones_where(
@@ -231,12 +230,11 @@
             far_t[at * SLOT : (at + 1) * SLOT, cols] = ones_where(offset == source * SLOT)
         far_t[HALO - SLOT :, cols] = jnp.zeros((SLOT, LANES), BF16)
 
-    loads[6].wait()
+    loads[4].wait()
     received = dot(xv[...], w[RECEIVE]).astype(BF16)
     loc_x[...] = dot(near[...], jnp.concatenate([sent[:OWN], received[:OWN]], axis=0))
     loc_v[...] = dot(near[...], jnp.concatenate([sent[OWN:], received[OWN:]], axis=0))
-    for load in loads[7:]:
-        load.wait()
+    loads[5].wait()
     node = dot(xv[...], w[NODE])
     w_mi = dot(w[MESSAGE], w[INBOX]).astype(BF16)
     w_oo = dot_t(w[OUTPUT], w[OUTPUT]).astype(BF16)
@@ -266,7 +264,7 @@
     edge_in = dot_t(node_bar, w_mi).astype(BF16)
     act[...] = (slope[...] * dot(near[:, OWN:], edge_in)).astype(BF16)
     half = HALO // 2
-    for at in (0, half):
+    for at in (half, 0):
         ret_out[at : at + half, :] = dot(far_t[at : at + half, :], act[...]).astype(BF16)
         for b in range(at // SLOT, min((at + half) // SLOT, len(AWAY))):
             send(block(ret_out, b), part(ret_in, me), 2, {"mesh": sources[b]})
@@ -346,8 +344,7 @@
         scratch_shapes=[
             rows(2 * OWN),
             pltpu.VMEM((6, WIDTH, WIDTH), BF16),
-            pltpu.VMEM((EDGES // LANES, LANES), jnp.int32),
-            pltpu.VMEM((EDGES // LANES, LANES), jnp.int32),
+            pltpu.VMEM((2, EDGES // LANES, LANES), jnp.int32),
             pltpu.VMEM((HALO // LANES, LANES), jnp.int32),
             pltpu.VMEM((HALO, OWN), BF16),
             pltpu.VMEM((OWN, HALO), BF16),
@@ -368,7 +365,7 @@
             pltpu.VMEM((EDGES, WIDTH), F32),
             pltpu.VMEM((EDGES, WIDTH), F32),
             pltpu.VMEM((EDGES, WIDTH), BF16),
-            pltpu.SemaphoreType.DMA((11,)),
+            pltpu.SemaphoreType.DMA((6,)),
             pltpu.SemaphoreType.DMA((5,)),
             pltpu.SemaphoreType.DMA((5,)),
         ],

time: 23.7 us -> 23.5 us (level)
  no operation moved by 1% of the time
where the time goes in v3:
time: 23.5 us
  Pallas kernels  22.8 us (97%)
  between operations  0.64 us (3%)
    pallas_call x1, Pallas kernels, on_device(): pl.pallas_call(kernel, out_shape=(pltpu.VMEM(image.shape, BF16),) * 2, in...  22.1 us
    pallas_call x1, Pallas kernels, on_device(): pl.pallas_call(store, out_shape=(image, image), in_specs=[pl.BlockSpec(me...  0.74 us

profile of v3, /device:TPU:96, one launch (start us, length us, event | category | flops | bytes accessed | tf_op | source)
XLA Modules:
  0.0 23.5 jit_solution(3790960421866964627)
XLA Ops:
  0.6 22.1 %shard_map.122 = (bf16[1,160,512]{2,1,0:T(8,128)(2,1)S(1)}, bf16[1,160,512]{2,1,0:T(8,128)(2,1)S(1)}) custom-call(bf16[1,160,512]{2,1,0:T(8,128)(2,1)} %x_hbm.1, bf16[1,160,512]{2,1,0:T(8,128)(2,1)} %v_hbm.1, bf16[512,512]{1,0:T(8,128)(2,1)} %ws_hbm.1, bf16[512,512]{1,0:T(8,128)(2,1)} %wr_hbm.1, bf16[512,512]{1,0:T(8,128)(2,1)} %wm_hbm.1, ...), custom_call_target="tpu_custom_call" | custom-call | tf_op jit(solution)/shard_map/pallas_call | solution.py:339
  22.7 0.7 %shard_map.123 = (bf16[1,160,512]{2,1,0:T(8,128)(2,1)}, bf16[1,160,512]{2,1,0:T(8,128)(2,1)}) custom-call(bf16[1,160,512]{2,1,0:T(8,128)(2,1)S(1)} %get-tuple-element.4.fi_vmem, bf16[1,160,512]{2,1,0:T(8,128)(2,1)S(1)} %get-tuple-element.5.ni_vmem), custom_call_target="tpu_custom_call" | custom-call | tf_op jit(solution)/shard_map/pallas_call | solution.py:376

commit v4 on v3

--- a/solution.py
+++ b/solution.py
@@ -82,6 +82,7 @@
     loc_v,
     slope,
     act,
+    turned,
     load_sem,
     send_sem,
     recv_sem,
@@ -237,6 +238,8 @@
     loads[5].wait()
     node = dot(xv[...], w[NODE])
     w_mi = dot(w[MESSAGE], w[INBOX]).astype(BF16)
+    turned[0] = w_mi.T
+    turned[1] = w[SEND].T
     w_oo = dot_t(w[OUTPUT], w[OUTPUT]).astype(BF16)
 
     all_x.wait_recv()
@@ -261,7 +264,7 @@
     node_tangent = (node_slope * (node[OWN:] + dot(tangent_sum, w_mi))).astype(BF16)
     node_bar = node_slope * (step_bar - dot(node_tangent, w_oo))
     node_bar = jnp.where(last, 0.0, node_bar).astype(BF16)
-    edge_in = dot_t(node_bar, w_mi).astype(BF16)
+    edge_in = dot(node_bar, turned[0]).astype(BF16)
     act[...] = (slope[...] * dot(near[:, OWN:], edge_in)).astype(BF16)
     half = HALO // 2
     for at in (half, 0):
@@ -288,7 +291,7 @@
 
     all_back.wait_recv()
     owned = (sums[:OWN] + dot(pick_t[...], ret_in[...])).astype(BF16)
-    ni_ref[0] = (rest - dot_t(owned, w[SEND])).astype(BF16)
+    ni_ref[0] = (rest - dot(owned, turned[1])).astype(BF16)
 
     all_x.wait_send()
     all_v.wait_send()
@@ -365,6 +368,7 @@
             pltpu.VMEM((EDGES, WIDTH), F32),
             pltpu.VMEM((EDGES, WIDTH), F32),
             pltpu.VMEM((EDGES, WIDTH), BF16),
+            pltpu.VMEM((2, WIDTH, WIDTH), BF16),
             pltpu.SemaphoreType.DMA((6,)),
             pltpu.SemaphoreType.DMA((5,)),
             pltpu.SemaphoreType.DMA((5,)),

time: 23.5 us -> 23.5 us (level)
  no operation moved by 1% of the time
where the time goes in v4:
time: 23.5 us; the launch traced here: 23.4 us
  Pallas kernels  22.7 us (97%)
  between operations  0.64 us (3%)
    pallas_call x1, Pallas kernels, on_device(): pl.pallas_call(kernel, out_shape=(pltpu.VMEM(image.shape, BF16),) * 2, in...  22 us
    pallas_call x1, Pallas kernels, on_device(): pl.pallas_call(store, out_shape=(image, image), in_specs=[pl.BlockSpec(me...  0.74 us

profile of v4, /device:TPU:96, one launch (start us, length us, event | category | flops | bytes accessed | tf_op | source)
XLA Modules:
  0.0 23.4 jit_solution(6189658970336981348)
XLA Ops:
  0.6 22.0 %shard_map.122 = (bf16[1,160,512]{2,1,0:T(8,128)(2,1)S(1)}, bf16[1,160,512]{2,1,0:T(8,128)(2,1)S(1)}) custom-call(bf16[1,160,512]{2,1,0:T(8,128)(2,1)} %x_hbm.1, bf16[1,160,512]{2,1,0:T(8,128)(2,1)} %v_hbm.1, bf16[512,512]{1,0:T(8,128)(2,1)} %ws_hbm.1, bf16[512,512]{1,0:T(8,128)(2,1)} %wr_hbm.1, bf16[512,512]{1,0:T(8,128)(2,1)} %wm_hbm.1, ...), custom_call_target="tpu_custom_call" | custom-call | tf_op jit(solution)/shard_map/pallas_call | solution.py:342
  22.6 0.7 %shard_map.123 = (bf16[1,160,512]{2,1,0:T(8,128)(2,1)}, bf16[1,160,512]{2,1,0:T(8,128)(2,1)}) custom-call(bf16[1,160,512]{2,1,0:T(8,128)(2,1)S(1)} %get-tuple-element.4.fi_vmem, bf16[1,160,512]{2,1,0:T(8,128)(2,1)S(1)} %get-tuple-element.5.ni_vmem), custom_call_target="tpu_custom_call" | custom-call | tf_op jit(solution)/shard_map/pallas_call | solution.py:380
